TPU v7x, 256 devices: a whole 4x4x8 slice. The times are simulated.
256 devices in a mesh: docs: 32 (over z, y_lo, core), layer: 8 (over y_hi, x).
Axes of the slice: x: 4, y: 4 (y_hi: 2, y_lo: 2; y = y_hi * 2 + y_lo), z: 8, core: 2. Of those that a mesh axis runs over, the one named last changes fastest.
Arguments:
- grad_out: bfloat16 [3584, 8, 32, 256], P('docs', 'layer')
- acts: bfloat16 [3584, 8, 256, 128], P('docs', 'layer')
- lengths: int32 [3584], P('docs'), may hold values from 64 to 256
Outputs:
- kernel: float32 [3584, 3584], P('docs', 'layer')
All inputs are finite; a program needn't handle non-finite values.
Results may differ from a plain program's by a relative error of at most 0.00064.
Values may be sent and summed in bfloat16 or wider, within the bound.
A program may use at most 128 MiB of HBM per device.

v0:
```python
import jax
import jax.numpy as jnp
from jax import lax
from jax.sharding import PartitionSpec as P

epsilon = 1e-06


def local(grad_out, acts, lengths):
    slots = lax.broadcasted_iota(jnp.int32, (lengths.shape[0], acts.shape[2]), 1)
    valid = (slots < lengths[:, None]).astype(jnp.bfloat16)
    masked = acts * valid[:, None, :, None]
    feature = jnp.einsum("dlot,dlti->dloi", grad_out, masked, preferred_element_type=jnp.float32)
    feature = feature.reshape(feature.shape[0], -1)
    squares = lax.psum(jnp.sum(feature * feature, axis=1), "layer")
    unit = (feature * lax.rsqrt(squares + epsilon)[:, None]).astype(jnp.bfloat16)
    kernel_part = lax.dot_general(
        unit,
        lax.all_gather(unit, "docs", axis=0, tiled=True),
        (((1,), (1,)), ((), ())),
        preferred_element_type=jnp.float32,
    )
    return lax.psum_scatter(kernel_part, "layer", scatter_dimension=1, tiled=True)


def solution(mesh):
    placed = (P("docs", "layer", None, None), P("docs", "layer", None, None), P("docs"))
    return jax.shard_map(
        local, mesh=mesh, in_specs=placed, out_specs=P("docs", "layer"), check_vma=False
    )
```

profile of v0, /device:TPU:16, one launch (start us, length us, event | category | flops | bytes accessed | tf_op | source)
XLA Modules:
  0.0 307.5 jit_solution(4947407762339881685)
XLA Ops:
  6.5 0.0 copy-start
  6.5 0.0 all-gather.2.cloned.1.call-start
  6.5 0.9 fusion.7
  7.4 0.6 copy-done
  8.1 7.7 %fusion.5 = (f32[112]{0:T(128)S(1)}, f32[112,128,32]{1,2,0:T(8,128)}) fusion(bf16[112,1,256,128]{3,2,1,0:T(8,128)(2,1)} %param.4, bf16[112,256]{1,0:T(8,128)(2,1)S(1)} %fusion.7, bf16[112,1,32,256]{3,2,1,0:T(8,128)(2,1)S(1)} %copy-done), kind=kOutput, calls=%fused_computation.8 | convolution fusion | flops 250478480 | bytes 11067840 | tf_op jit(solution)/shard_map/dlot,dlti->dloi/dot_general | solution.py:13
  15.7 21.5 %psum.7 = f32[112]{0:T(128)S(1)} all-reduce(f32[112]{0:T(128)S(1)} %get-tuple-element.5), channel_id=1, replica_groups=mesh['docs'=32,'layer'=8] {'layer'}, use_global_device_ids=true, to_apply=%region_1.0 | all-reduce | flops 112 | bytes 896 | tf_op jit(solution)/shard_map/psum | solution.py:15
  37.2 3.5 %fusion.4 = bf16[112,4096]{1,0:T(8,128)(2,1)} fusion(f32[14,8,32,128]{3,2,1,0:T(8,128)} %bitcast.24, f32[112]{0:T(128)S(1)} %add_rsqrt_fusion), kind=kLoop, calls=%fused_computation.6 | loop fusion | flops 917504 | bytes 2752960 | tf_op jit(solution)/shard_map/convert_element_type | solution.py:16
  40.6 0.0 all-gather.2.cloned.1.call-update
  40.7 0.0 reduce-scatter.4.cloned.1.call-start
  40.7 164.2 %all-gather.2.cloned.1.call-done = bf16[3584,4096]{1,0:T(8,128)(2,1)} async-done(((bf16[112,4096]{1,0:T(8,128)(2,1)}), bf16[3584,4096]{1,0:T(8,128)(2,1)}) %all-gather.2.cloned.1.call-update) | async-done | bytes 29360144 | tf_op jit(solution)/shard_map/all_gather | solution.py:19
  205.0 14.5 %convolution_bitcast_fusion = f32[3584,112]{1,0:T(8,128)} fusion(bf16[112,4096]{1,0:T(8,128)(2,1)} %fusion.4, bf16[3584,4096]{1,0:T(8,128)(2,1)} %all-gather.2.cloned.1.call-done), kind=kOutput, calls=%fused_computation.3 | convolution fusion | flops 3288334336 | bytes 31883264
  219.5 0.0 reduce-scatter.4.cloned.1.call-update
  219.5 79.4 %reduce-scatter.4.cloned.1.call-done = f32[448,112]{1,0:T(8,128)} async-done(((f32[3584,112]{1,0:T(8,128)}), f32[448,112]{1,0:T(8,128)}) %reduce-scatter.4.cloned.1.call-update) | async-done | bytes 200720
  298.9 1.8 copy.5
  (1 shorter events, 0.0 us)
Async XLA Ops:
  6.5 1.5 copy-start
  6.5 198.4 %all-gather.2.cloned.1.call-start = ((), (), s32[]{:S(2)}) async-start(), calls=%async_computation.1 | async-start | bytes 30277632 | tf_op jit(solution)/shard_map/all_gather | solution.py:19
  40.7 258.3 %reduce-scatter.4.cloned.1.call-start = ((), (), s32[]{:S(2)}) async-start(), calls=%async_computation.2 | async-start | bytes 2064384
Sparse Core Ops, SparseCore 0:
  40.8 164.1 all-gather.1
  219.6 79.2 reduce-scatter.3
where the time goes:
time: 309 us; the launch traced here: 308 us
  waiting for transfers between devices  244 us (79%)
  matrix products  22.2 us (7%)
  blocking collectives  21.5 us (7%)
  between operations  13.4 us (4%)
  other arithmetic  4.34 us (1%)
    all_gather x1, waiting for transfers between devices, local(): lax.all_gather(unit, 'docs', axis=0, tiled=True)  164 us
    unnamed x3, waiting for transfers between devices  79.5 us
    psum x1, blocking collectives, local(): squares = lax.psum(jnp.sum(feature * feature, axis=1), 'layer')  21.5 us
    unnamed x1, matrix products  14.5 us
    dot_general x1, matrix products, local(): jnp.einsum('dlot,dlti->dloi', grad_out, masked, preferred_element_type=jn...  7.65 us
  transfers between devices with their start and end apart: 2, of which 2 were waited for; matrix products, arithmetic and copies ran while one was open for 0% of the time, Pallas kernels for 0%

commit v1 on v0

v1 whole, which is shorter than its diff:
```python
import functools

import jax
import jax.numpy as jnp
from jax import lax
from jax.experimental import pallas as pl
from jax.experimental.pallas import tpu as pltpu
from jax.sharding import PartitionSpec as P

epsilon = 1e-06
MESH = pl.DeviceIdType.MESH
F32 = jnp.float32
BF16 = jnp.bfloat16

DB = 112
KO = 32
KI = 128
SEQ = 256
NZ = 8
CH = 16
GO = 8
PR = 56


def body(
    lengths_ref, grad_hbm, acts_hbm, out_ref,
    gbuf, abuf, feat, S, R, PP, RR, V, L, T, sq, sqr,
    in_sem, qs, qr, zs, zr, ys, yr, cs, cr, rs, rr, ls, ts, lr, tr,
):
    d = lax.axis_index("docs")
    me_l = lax.axis_index("layer")
    z, yl, c = d // 4, (d // 2) % 2, d % 2
    me = yl * 2 + c
    yme = (1 - yl) * 2 + c

    def dev(zz, slot, ll):
        return (zz * 4 + slot, ll)

    up = dev(lax.rem(z + 1, NZ), me, me_l)
    down = dev(lax.rem(z + NZ - 1, NZ), me, me_l)
    ypart = dev(z, yme, me_l)
    cpart = dev(z, yl * 2 + 1 - c, me_l)
    self_final = (me_l // 2) == me

    def rcopy(src, dst, ss, rs_, to):
        return pltpu.make_async_remote_copy(
            src_ref=src, dst_ref=dst, send_sem=ss, recv_sem=rs_, device_id=to, device_id_type=MESH
        )

    chunks = DB // CH
    def in_copies(k):
        rows = pl.ds(k * CH, CH)
        return (
            pltpu.make_async_copy(grad_hbm.at[rows], gbuf.at[rows], in_sem.at[0, k]),
            pltpu.make_async_copy(acts_hbm.at[rows], abuf.at[rows], in_sem.at[1, k]),
        )
    for k in range(chunks):
        for copy in in_copies(k):
            copy.start()

    barrier = pltpu.get_barrier_semaphore()
    def hello(to):
        pl.semaphore_signal(barrier, inc=1, device_id=to, device_id_type=MESH)
    for to in (up, down, ypart, cpart):
        hello(to)
    @pl.loop(1, NZ)
    def _(p):
        hello(dev(z, me, lax.rem(me_l + p, NZ)))
    @pl.loop(0, 8)
    def _(i):
        ll = 2 * me + i // 4
        slot = i % 4
        @pl.when(jnp.logical_not((ll == me_l) & (slot == me)))
        def _():
            hello(dev(z, slot, ll))
    @pl.when(me_l != z)
    def _():
        @pl.loop(0, NZ)
        def _(g):
            hello(dev(me_l, me, g))

    @pl.loop(0, chunks)
    def _(k):
        for copy in in_copies(k):
            copy.wait()
        @pl.loop(0, CH, unroll=4)
        def _(j):
            doc = k * CH + j
            n = lengths_ref[doc]
            slots = lax.broadcasted_iota(jnp.int32, (KO, SEQ), 1)
            valid = (slots < n).astype(F32).astype(BF16)
            feat[pl.ds(pl.multiple_of(doc * KO, KO), KO), :] = jnp.dot(
                gbuf[doc] * valid, abuf[doc], preferred_element_type=F32
            )

    acc = jnp.zeros((DB, KI), F32)
    for o in range(KO):
        x = feat[pl.ds(o, DB, stride=KO), :]
        acc = acc + x * x
    eye = lax.broadcasted_iota(jnp.int32, (DB, KI), 0) == lax.broadcasted_iota(jnp.int32, (DB, KI), 1)
    col = jnp.broadcast_to(jnp.sum(acc, axis=1, keepdims=True), (DB, KI))
    row = jnp.sum(jnp.where(eye, col, 0.0), axis=0, keepdims=True)
    sq[...] = jnp.broadcast_to(row, (8, KI))

    pl.semaphore_wait(barrier, 4 + 7 + 8 + 7 - self_final.astype(jnp.int32))

    def sq_copy(p):
        return rcopy(sq, sqr.at[p - 1], qs.at[p - 1], qr.at[p - 1], dev(z, me, lax.rem(me_l + p, NZ)))
    @pl.loop(1, NZ)
    def _(p):
        sq_copy(p).start()
    PP[...] = jnp.zeros_like(PP)
    @pl.when(me_l == z)
    def _():
        T[...] = jnp.zeros_like(T)
    @pl.loop(1, NZ)
    def _(p):
        sq_copy(p).wait()
    total = sq[0:1, :]
    for p in range(NZ - 1):
        total = total + sqr[p, 0:1, :]
    scale = jnp.sum(jnp.where(eye, jnp.broadcast_to(total, (DB, KI)), 0.0), axis=1, keepdims=True)
    scale = jnp.broadcast_to(lax.rsqrt(scale + epsilon), (DB, KI))

    def slot_of(h, sub, direction):
        return (h - 1) * 4 + sub * 2 + direction

    def z_copy(h, sub, direction):
        kc = direction * 2 + sub
        src = S.at[kc, me] if h == 1 else R.at[slot_of(h - 1, sub, direction)]
        to = (up, down)[direction]
        if h == 4:
            return rcopy(src, R.at[12 + direction], zs.at[direction, 3, 0], zr.at[direction, 3, 0], to)
        return rcopy(
            src, R.at[slot_of(h, sub, direction)], zs.at[direction, h - 1, sub], zr.at[direction, h - 1, sub], to
        )

    def y_copy(kc):
        return rcopy(S.at[kc, me], S.at[kc, me], ys.at[kc], yr.at[kc], ypart)

    def c_copy(which, kc):
        slot = (me, yme)[which]
        return rcopy(S.at[kc, slot], S.at[kc, slot], cs.at[which, kc], cr.at[which, kc], cpart)

    order = (0, 2, 1, 3)
    for kc in order:
        for j in range(GO):
            x = feat[pl.ds(kc * GO + j, DB, stride=KO), :]
            S[kc, me, j] = (x * scale).astype(BF16)
        z_copy(1, kc % 2, kc // 2).start()
        y_copy(kc).start()
        c_copy(0, kc).start()

    def product(kc, xs):
        right = jnp.concatenate([xs[j] for j in range(GO)], axis=1)
        right = jnp.concatenate([right, jnp.zeros((KI - DB, GO * KI), BF16)], axis=0)
        left = jnp.concatenate(
            [jnp.concatenate([S[kc, r, j] for j in range(GO)], axis=1) for r in range(4)], axis=0
        )
        res = lax.dot_general(left, right, (((1,), (1,)), ((), ())), preferred_element_type=F32)
        return res.reshape(8, PR, KI)

    def multiply(i):
        h1, sub, direction = i // 4, (i // 2) % 2, i % 2
        PP[2 * h1 + direction] += product(direction * 2 + sub, R.at[i])

    def r_copy(b, p):
        to = lax.rem(me_l + p, NZ)
        return rcopy(PP.at[b, to], RR.at[b, p - 1], rs.at[b, p - 1], rr.at[b, p - 1], dev(z, me, to))

    def send_partials(b):
        @pl.loop(1, NZ)
        def _(p):
            r_copy(b, p).start()

    def plane_of(b):
        h = b // 2 + 1
        other = jnp.where(b % 2 == 0, z + NZ - h, z + h)
        return lax.rem(jnp.where(b == 7, z, jnp.where(b == 6, z + 4, other)), NZ)

    def l_copy(b):
        return rcopy(V.at[b], L.at[me, me_l % 2], ls.at[b], lr.at[me, me_l % 2], dev(z, me_l // 2, plane_of(b)))

    def l_copy_self(b):
        return pltpu.make_async_copy(V.at[b], L.at[me, me_l % 2], lr.at[me, me_l % 2])

    def t_copy(b):
        return rcopy(V.at[b], T.at[me_l], ts.at[b], tr.at[me_l], dev(plane_of(b), me, z))

    def finish(b):
        total = PP[b, me_l]
        for p in range(1, NZ):
            r_copy(b, p).wait_recv()
            total = total + RR[b, p - 1]
        V[b] = total
        to_self = self_final & (plane_of(b) == me_l)
        @pl.when(to_self)
        def _():
            l_copy_self(b).start()
        @pl.when(jnp.logical_not(to_self))
        def _():
            l_copy(b).start()
        @pl.when(b != 7)
        def _():
            t_copy(b).start()

    far = (lax.rem(z + NZ - 3, NZ) // 4, lax.rem(z + 3, NZ) // 4)
    arriving = lax.rem(z + 4, NZ) // 4

    for tick in range(6):
        h, sub = tick // 2 + 1, tick % 2
        for direction in range(2):
            z_copy(h, sub, direction).wait_recv()
            if h < 3:
                z_copy(h + 1, sub, direction).start()
            else:
                @pl.when(far[direction] == sub)
                def _():
                    z_copy(4, sub, direction).start()
        if tick < 4:
            kc = order[tick]
            y_copy(kc).wait_recv()
            c_copy(1, kc).start()
        if 1 <= tick <= 4:
            kc = order[tick - 1]
            c_copy(0, kc).wait_recv()
            c_copy(1, kc).wait_recv()
            PP[7] += product(kc, S.at[kc, me])
        if tick == 4:
            send_partials(7)
            @pl.loop(0, 8)
            def _(i):
                multiply(i)
            @pl.loop(0, 4)
            def _(b):
                send_partials(b)
            @pl.loop(8, 10)
            def _(i):
                multiply(i)
        if tick == 5:
            @pl.loop(10, 12)
            def _(i):
                multiply(i)
            @pl.loop(4, 6)
            def _(b):
                send_partials(b)

    finish(7)
    @pl.loop(0, 4)
    def _(b):
        finish(b)

    for direction in range(2):
        z_copy(4, 0, direction).wait_recv()
        PP[6] += product(direction * 2 + arriving, R.at[12 + direction])
    send_partials(6)
    @pl.loop(4, 7)
    def _(b):
        finish(b)

    for h in range(1, 5):
        for sub in range(2 if h < 4 else 1):
            for direction in range(2):
                z_copy(h, sub, direction).wait_send()
    for kc in range(4):
        y_copy(kc).wait_send()
        c_copy(0, kc).wait_send()
        c_copy(1, kc).wait_send()
    @pl.loop(0, 8)
    def _(b):
        @pl.loop(1, NZ)
        def _(p):
            r_copy(b, p).wait_send()
        to_self = self_final & (plane_of(b) == me_l)
        @pl.when(jnp.logical_not(to_self))
        def _():
            l_copy(b).wait_send()
        @pl.when(b != 7)
        def _():
            t_copy(b).wait_send()

    for t in range(4):
        for half in range(2):
            rcopy(V.at[0], L.at[t, half], ls.at[0], lr.at[t, half], up).wait_recv()
    @pl.when(me_l != z)
    def _():
        for g in range(NZ):
            rcopy(V.at[0], T.at[g], ts.at[0], tr.at[g], up).wait_recv()
    own = jnp.concatenate([L[t].reshape(DB, KI)[:, :DB] for t in range(4)], axis=1)
    other = jnp.transpose(T[...].reshape(NZ * PR, KI))
    out_ref[...] = own + other[:DB, :]


def local(grad_out, acts, lengths):
    grads = grad_out.reshape(DB, KO, SEQ)
    inputs = acts.reshape(DB, SEQ, KI)
    dma = pltpu.SemaphoreType.DMA
    return pl.pallas_call(
        body,
        out_shape=jax.ShapeDtypeStruct((DB, 4 * DB), F32),
        in_specs=[
            pl.BlockSpec(memory_space=pltpu.SMEM),
            pl.BlockSpec(memory_space=pl.ANY),
            pl.BlockSpec(memory_space=pl.ANY),
        ],
        out_specs=pl.BlockSpec(memory_space=pltpu.VMEM),
        scratch_shapes=[
            pltpu.VMEM((DB, KO, SEQ), BF16),
            pltpu.VMEM((DB, SEQ, KI), BF16),
            pltpu.VMEM((DB * KO, KI), F32),
            pltpu.VMEM((4, 4, GO, DB, KI), BF16),
            pltpu.VMEM((14, GO, DB, KI), BF16),
            pltpu.VMEM((8, 8, PR, KI), F32),
            pltpu.VMEM((8, 7, PR, KI), F32),
            pltpu.VMEM((8, PR, KI), F32),
            pltpu.VMEM((4, 2, PR, KI), F32),
            pltpu.VMEM((8, PR, KI), F32),
            pltpu.VMEM((8, KI), F32),
            pltpu.VMEM((7, 8, KI), F32),
            dma((2, DB // CH)),
            dma((7,)), dma((7,)),
            dma((2, 4, 2)), dma((2, 4, 2)),
            dma((4,)), dma((4,)),
            dma((2, 4)), dma((2, 4)),
            dma((8, 7)), dma((8, 7)),
            dma((8,)), dma((8,)),
            dma((4, 2)), dma((8,)),
        ],
        compiler_params=pltpu.CompilerParams(
            collective_id=0, has_side_effects=True, vmem_limit_bytes=48 * 2**20
        ),
    )(lengths, grads, inputs)


def solution(mesh):
    placed = (P("docs", "layer", None, None), P("docs", "layer", None, None), P("docs"))
    return jax.shard_map(
        local, mesh=mesh, in_specs=placed, out_specs=P("docs", "layer"), check_vma=False
    )
```

time: 309 us -> 91.6 us (0.30)
  waiting for transfers between devices: 244 us -> 0 us
  Pallas kernels: 0 us -> 88.7 us
  matrix products: 22.2 us -> 0 us
  blocking collectives: 21.5 us -> 0 us
  between operations: 13.4 us -> 0.01 us
  other arithmetic: 4.34 us -> 0 us
    all_gather x1 -> x0, waiting for transfers between devices: 164 us -> none  [local(): lax.all_gather(unit, 'docs', axis=0, tiled=True)]
    pallas_call x0 -> x1, Pallas kernels: none -> 88.7 us  [local(): pl.pallas_call(body, out_shape=jax.ShapeDtypeStruct((DB, 4 * DB), F32), i...]
    unnamed x3 -> x0, waiting for transfers between devices: 79.5 us -> none
    psum x1 -> x0, blocking collectives: 21.5 us -> none  [local(): squares = lax.psum(jnp.sum(feature * feature, axis=1), 'layer')]
    unnamed x1 -> x0, matrix products: 14.5 us -> none
    dot_general x1 -> x0, matrix products: 7.65 us -> none  [local(): jnp.einsum('dlot,dlti->dloi', grad_out, masked, preferred_element_type=jn...]
    convert_element_type x2 -> x0, other arithmetic: 4.33 us -> none  [the longest x1 3.47 us: local(): (feature * lax.rsqrt(squares + epsilon)[:, None]).astype(jnp.bfloat16)]
  transfers between devices with their start and end apart: 2 -> 0, of which waited for: 2 -> 0; matrix products, arithmetic and copies ran while one was open for 0% -> 0% of each run, Pallas kernels for 0% -> 0%
where the time goes in v1:
time: 91.6 us; the launch traced here: 91.5 us
  Pallas kernels  88.7 us (97%)
  local copies, waits for them, and re-layouts  2.84 us (3%)
    pallas_call x1, Pallas kernels, local(): pl.pallas_call(body, out_shape=jax.ShapeDtypeStruct((DB, 4 * DB), F32), i...  88.7 us
    unnamed x5, local copies, waits for them, and re-layouts  2.84 us

profile of v1, /device:TPU:16, one launch (start us, length us, event | category | flops | bytes accessed | tf_op | source)
XLA Modules:
  0.0 91.5 jit_solution(17902778336751168000)
XLA Ops:
  0.0 0.0 copy-start
  0.0 1.5 %copy-done = bf16[112,1,32,256]{3,2,1,0:T(8,128)(2,1)S(1)} copy-done((bf16[112,1,32,256]{3,2,1,0:T(8,128)(2,1)S(1)}, bf16[112,1,32,256]{3,2,1,0:T(8,128)(2,1)}, u32[]{:S(2)}) %copy-start) | copy-done | bytes 1835032
  1.5 0.0 copy-start.1
  1.5 0.7 copy-done.1
  2.2 88.7 %shard_map.37 = f32[112,448]{1,0:T(8,128)S(1)} custom-call(s32[112]{0:T(128)S(1)} %copy-done.1, bf16[112,32,256]{2,1,0:T(8,128)(2,1)S(1)} %bitcast.2, bf16[112,256,128]{2,1,0:T(8,128)(2,1)} %bitcast.3), custom_call_target="tpu_custom_call" | custom-call | tf_op jit(solution)/shard_map/pallas_call | solution.py:298
  90.8 0.7 copy.5
Async XLA Ops:
  0.0 1.5 %copy-start = (bf16[112,1,32,256]{3,2,1,0:T(8,128)(2,1)S(1)}, bf16[112,1,32,256]{3,2,1,0:T(8,128)(2,1)}, u32[]{:S(2)}) copy-start(bf16[112,1,32,256]{3,2,1,0:T(8,128)(2,1)} %param.3) | copy-start | bytes 5505028
  1.5 0.7 copy-start.1

commit v2 on v1

v2 whole, which is shorter than its diff:
```python
import functools

import jax
import jax.numpy as jnp
from jax import lax
from jax.experimental import pallas as pl
from jax.experimental.pallas import tpu as pltpu
from jax.sharding import PartitionSpec as P

epsilon = 1e-06
MESH = pl.DeviceIdType.MESH
F32 = jnp.float32
BF16 = jnp.bfloat16

DB = 112
KO = 32
KI = 128
SEQ = 256
NZ = 8
CH = 16
GO = 8
PR = 56


def body(
    lengths_ref, grad_hbm, acts_hbm, out_ref,
    gbuf, abuf, feat, S, R, PP, RR, XS, RY, V, L, T, sq, sqr, norm, norms,
    in_sem, qs, qr, ns, nr, zs, zr, ys, yr, cs, cr, rs, rr, ps, pr, ls, ts, lr, tr,
):
    d = lax.axis_index("docs")
    me_l = lax.axis_index("layer")
    z, yl, c = d // 4, (d // 2) % 2, d % 2
    yh, x = me_l // 4, me_l % 4
    me = yl * 2 + c
    yme = (1 - yl) * 2 + c

    def dev(zz, slot, ll):
        return (zz * 4 + slot, ll)

    up = dev(lax.rem(z + 1, NZ), me, me_l)
    down = dev(lax.rem(z + NZ - 1, NZ), me, me_l)
    ypart = dev(z, yme, me_l)
    cpart = dev(z, yl * 2 + 1 - c, me_l)
    self_final = (me_l // 2) == me
    diagonal = me_l == z

    def rcopy(src, dst, ss, rs_, to):
        return pltpu.make_async_remote_copy(
            src_ref=src, dst_ref=dst, send_sem=ss, recv_sem=rs_, device_id=to, device_id_type=MESH
        )

    chunks = DB // CH
    def in_copies(k):
        rows = pl.ds(k * CH, CH)
        return (
            pltpu.make_async_copy(grad_hbm.at[rows], gbuf.at[rows], in_sem.at[0, k]),
            pltpu.make_async_copy(acts_hbm.at[rows], abuf.at[rows], in_sem.at[1, k]),
        )
    for k in range(chunks):
        for copy in in_copies(k):
            copy.start()

    barrier = pltpu.get_barrier_semaphore()
    def hello(to):
        pl.semaphore_signal(barrier, inc=1, device_id=to, device_id_type=MESH)
    for to in (up, down, ypart, cpart):
        hello(to)
    @pl.loop(1, NZ)
    def _(p):
        hello(dev(z, me, lax.rem(me_l + p, NZ)))
    @pl.loop(0, 8)
    def _(i):
        ll = 2 * me + i // 4
        slot = i % 4
        @pl.when(jnp.logical_not((ll == me_l) & (slot == me)))
        def _():
            hello(dev(z, slot, ll))
    @pl.when(jnp.logical_not(diagonal))
    def _():
        @pl.loop(0, NZ)
        def _(g):
            hello(dev(me_l, me, g))
    @pl.loop(0, 4)
    def _(t):
        @pl.when(jnp.logical_not(diagonal & (t == me)))
        def _():
            hello(dev(me_l, t, z))

    @pl.loop(0, chunks)
    def _(k):
        for copy in in_copies(k):
            copy.wait()
        @pl.loop(0, CH, unroll=CH)
        def _(j):
            doc = k * CH + j
            n = lengths_ref[doc]
            slots = lax.broadcasted_iota(jnp.int32, (KO, SEQ), 1)
            valid = (slots < n).astype(F32).astype(BF16)
            feat[pl.ds(pl.multiple_of(doc * KO, KO), KO), :] = jnp.dot(
                gbuf[doc] * valid, abuf[doc], preferred_element_type=F32
            )

    pl.semaphore_wait(barrier, 4 + 7 + 8 + 7 + 4 - self_final.astype(jnp.int32) - diagonal.astype(jnp.int32))

    def slot_of(h, sub, direction):
        return (h - 1) * 4 + sub * 2 + direction

    def z_copy(h, sub, direction):
        kc = direction * 2 + sub
        src = S.at[kc, me] if h == 1 else R.at[slot_of(h - 1, sub, direction)]
        to = (up, down)[direction]
        if h == 4:
            return rcopy(src, R.at[12 + direction], zs.at[direction, 3, 0], zr.at[direction, 3, 0], to)
        return rcopy(
            src, R.at[slot_of(h, sub, direction)], zs.at[direction, h - 1, sub], zr.at[direction, h - 1, sub], to
        )

    def y_copy(kc):
        return rcopy(S.at[kc, me], S.at[kc, me], ys.at[kc], yr.at[kc], ypart)

    def c_copy(which, kc):
        slot = (me, yme)[which]
        return rcopy(S.at[kc, slot], S.at[kc, slot], cs.at[which, kc], cr.at[which, kc], cpart)

    order = (0, 2, 1, 3)
    acc = jnp.zeros((DB, KI), F32)
    for kc in order:
        for j in range(GO):
            values = feat[pl.ds(kc * GO + j, DB, stride=KO), :]
            acc = acc + values * values
            S[kc, me, j] = values.astype(BF16)
        z_copy(1, kc % 2, kc // 2).start()
        c_copy(0, kc).start()

    eye = lax.broadcasted_iota(jnp.int32, (DB, KI), 0) == lax.broadcasted_iota(jnp.int32, (DB, KI), 1)
    def as_column(row):
        wide = jnp.where(eye, jnp.broadcast_to(row, (DB, KI)), 0.0)
        return jnp.broadcast_to(jnp.sum(wide, axis=1, keepdims=True), (DB, KI))
    column = jnp.broadcast_to(jnp.sum(acc, axis=1, keepdims=True), (DB, KI))
    row = jnp.sum(jnp.where(eye, column, 0.0), axis=0, keepdims=True)
    sq[...] = jnp.broadcast_to(row, (8, KI))

    def sq_copy(p):
        return rcopy(sq, sqr.at[p - 1], qs.at[p - 1], qr.at[p - 1], dev(z, me, lax.rem(me_l + p, NZ)))
    @pl.loop(1, NZ)
    def _(p):
        sq_copy(p).start()
    for kc in order:
        y_copy(kc).start()
    PP[...] = jnp.zeros_like(PP)
    @pl.when(diagonal)
    def _():
        T[...] = jnp.zeros_like(T)
    def norm_copy(t):
        return rcopy(norm, norms.at[me], ns.at[t], nr.at[me], dev(me_l, t, z))
    def other_slots(act):
        @pl.loop(0, 4)
        def _(t):
            @pl.when(jnp.logical_not(diagonal & (t == me)))
            def _():
                act(t)
    def make_norms():
        @pl.loop(1, NZ)
        def _(p):
            sq_copy(p).wait()
        total = sq[0:1, :]
        for p in range(NZ - 1):
            total = total + sqr[p, 0:1, :]
        norm[...] = jnp.broadcast_to(lax.rsqrt(total + epsilon), (8, KI))
        @pl.when(diagonal)
        def _():
            norms[me] = norm[...]
        other_slots(lambda t: norm_copy(t).start())


    def product(kc, xs, pair):
        right = jnp.concatenate([xs[j] for j in range(GO)], axis=1)
        right = jnp.concatenate([right, jnp.zeros((KI - DB, GO * KI), BF16)], axis=0)
        left = jnp.concatenate(
            [jnp.concatenate([S[kc, 2 * pair + r, j] for j in range(GO)], axis=1) for r in range(2)], axis=0
        )
        res = lax.dot_general(left, right, (((1,), (1,)), ((), ())), preferred_element_type=F32)
        return res.reshape(4, PR, KI)

    def multiply(i, pair):
        h1, sub, direction = i // 4, (i // 2) % 2, i % 2
        PP[2 * h1 + direction, pl.ds(4 * pair, 4)] += product(direction * 2 + sub, R.at[i], pair)

    def multiply_own(kc, pair):
        PP[7, pl.ds(4 * pair, 4)] += product(kc, S.at[kc, me], pair)

    def r_copy(b, to):
        return rcopy(PP.at[b, to], RR.at[b, me_l], rs.at[b, to], rr.at[b, me_l], dev(z, me, to))

    def send_partials(b, pair):
        @pl.loop(0, 4)
        def _(q):
            to = 4 * pair + q
            @pl.when(to != me_l)
            def _():
                r_copy(b, to).start()

    def x_copy(b, pair, to):
        return rcopy(
            PP.at[b, 4 * pair + to], RR.at[b, 4 * pair + x], rs.at[b, 4 * pair + to], rr.at[b, 4 * pair + x],
            dev(z, me, 4 * yh + to),
        )

    def p_copy(b):
        return rcopy(XS.at[b], RY.at[b], ps.at[b], pr.at[b], dev(z, me, 4 * (1 - yh) + x))

    def send_over_x(b, pair):
        @pl.loop(1, 4)
        def _(p):
            x_copy(b, pair, lax.rem(x + p, 4)).start()

    def add_over_x(b, pair):
        total = PP[b, 4 * pair + x]
        for p in range(1, 4):
            slot = 4 * pair + lax.rem(x + p, 4)
            rcopy(PP.at[b, 0], RR.at[b, slot], rs.at[b, 0], rr.at[b, slot], up).wait_recv()
            total = total + RR[b, slot]
        @pl.when(pair == yh)
        def _():
            V[b] = total
        @pl.when(pair != yh)
        def _():
            XS[b] = total
            p_copy(b).start()

    def plane_of(b):
        h = b // 2 + 1
        other = jnp.where(b % 2 == 0, z + NZ - h, z + h)
        return lax.rem(jnp.where(b == 7, z, jnp.where(b == 6, z + 4, other)), NZ)

    def l_copy(b):
        return rcopy(V.at[b], L.at[me, me_l % 2], ls.at[b], lr.at[me, me_l % 2], dev(z, me_l // 2, plane_of(b)))

    def l_copy_self(b):
        return pltpu.make_async_copy(V.at[b], L.at[me, me_l % 2], lr.at[me, me_l % 2])

    def t_copy(b):
        return rcopy(V.at[b], T.at[me_l], ts.at[b], tr.at[me_l], dev(plane_of(b), me, z))

    def send_own(b):
        to_self = self_final & (plane_of(b) == me_l)
        @pl.when(to_self)
        def _():
            l_copy_self(b).start()
        @pl.when(jnp.logical_not(to_self))
        def _():
            l_copy(b).start()

    def add_two_steps(b):
        p_copy(b).wait_recv()
        V[b] = V[b] + RY[b]
        send_own(b)

    def add_up(b):
        total = PP[b, me_l]
        for p in range(1, NZ):
            source = lax.rem(me_l + p, NZ)
            rcopy(PP.at[b, 0], RR.at[b, source], rs.at[b, 0], rr.at[b, source], up).wait_recv()
            total = total + RR[b, source]
        V[b] = total
        send_own(b)
        t_copy(b).start()

    far = (lax.rem(z + NZ - 3, NZ) // 4, lax.rem(z + 3, NZ) // 4)
    arriving = lax.rem(z + 4, NZ) // 4

    def pass_on(tick):
        h, sub = tick // 2 + 1, tick % 2
        for direction in range(2):
            z_copy(h, sub, direction).wait_recv()
            if h < 3:
                z_copy(h + 1, sub, direction).start()
            else:
                @pl.when(far[direction] == sub)
                def _():
                    z_copy(4, sub, direction).start()
        if tick < 4:
            y_copy(order[tick]).wait_recv()
            c_copy(1, order[tick]).start()

    for kc in order:
        c_copy(0, kc).wait_recv()
        multiply_own(kc, yl)
    send_over_x(7, yl)

    pass_on(0)
    pass_on(1)
    @pl.loop(0, 4)
    def _(i):
        multiply(i, yl)
    @pl.loop(0, 2)
    def _(b):
        send_over_x(b, yl)
    make_norms()
    pass_on(2)
    pass_on(3)
    @pl.loop(4, 8)
    def _(i):
        multiply(i, yl)
    @pl.loop(2, 4)
    def _(b):
        send_over_x(b, yl)
    for kc in order:
        c_copy(1, kc).wait_recv()
    for kc in order:
        multiply_own(kc, 1 - yl)
    send_over_x(7, 1 - yl)
    @pl.loop(0, 2)
    def _(h1):
        @pl.loop(0, 4)
        def _(i):
            multiply(4 * h1 + i, 1 - yl)
        send_over_x(2 * h1, 1 - yl)
        send_over_x(2 * h1 + 1, 1 - yl)
    add_over_x(7, yl)
    @pl.loop(0, 4)
    def _(b):
        add_over_x(b, yl)
    pass_on(4)
    @pl.loop(0, 4)
    def _(i):
        multiply(8 + i // 2, i % 2)
    pass_on(5)
    @pl.loop(0, 4)
    def _(i):
        multiply(10 + i // 2, i % 2)
    @pl.loop(0, 4)
    def _(i):
        send_partials(4 + i // 2, i % 2)

    add_over_x(7, 1 - yl)
    @pl.loop(0, 4)
    def _(b):
        add_over_x(b, 1 - yl)
    add_two_steps(7)
    @pl.loop(0, 4)
    def _(b):
        add_two_steps(b)

    for direction in range(2):
        z_copy(4, 0, direction).wait_recv()
    for pair in range(2):
        for direction in range(2):
            PP[6, pl.ds(4 * pair, 4)] += product(direction * 2 + arriving, R.at[12 + direction], pair)
        send_partials(6, pair)
    @pl.loop(0, 4)
    def _(b):
        t_copy(b).start()
    @pl.loop(4, 7)
    def _(b):
        add_up(b)

    for h in range(1, 5):
        for sub in range(2 if h < 4 else 1):
            for direction in range(2):
                z_copy(h, sub, direction).wait_send()
    for kc in range(4):
        y_copy(kc).wait_send()
        c_copy(0, kc).wait_send()
        c_copy(1, kc).wait_send()
    other_slots(lambda t: norm_copy(t).wait_send())
    @pl.loop(0, 8)
    def _(b):
        direct = (b >= 4) & (b < 7)
        @pl.when(direct)
        def _():
            @pl.loop(0, NZ)
            def _(to):
                @pl.when(to != me_l)
                def _():
                    r_copy(b, to).wait_send()
        @pl.when(jnp.logical_not(direct))
        def _():
            @pl.loop(0, NZ)
            def _(i):
                @pl.when(i % 4 != x)
                def _():
                    x_copy(b, i // 4, i % 4).wait_send()
            p_copy(b).wait_send()
        to_self = self_final & (plane_of(b) == me_l)
        @pl.when(jnp.logical_not(to_self))
        def _():
            l_copy(b).wait_send()
        @pl.when(b != 7)
        def _():
            t_copy(b).wait_send()

    def norm_arrived(t):
        rcopy(norm, norms.at[t], ns.at[t], nr.at[t], up).wait_recv()
    other_slots(norm_arrived)
    for t in range(4):
        for half in range(2):
            rcopy(V.at[0], L.at[t, half], ls.at[0], lr.at[t, half], up).wait_recv()
    @pl.when(jnp.logical_not(diagonal))
    def _():
        for g in range(NZ):
            rcopy(V.at[0], T.at[g], ts.at[0], tr.at[g], up).wait_recv()
    own = jnp.concatenate([L[t].reshape(DB, KI)[:, :DB] for t in range(4)], axis=1)
    other = jnp.transpose(T[...].reshape(NZ * PR, KI))[:DB, :]
    rows = as_column(norm[0:1, :])
    rows = jnp.concatenate([rows, rows, rows, rows[:, : 4 * DB - 3 * KI]], axis=1)
    columns = jnp.concatenate([norms[t, 0:1, :DB] for t in range(4)], axis=1)
    columns = jnp.broadcast_to(columns, (DB, 4 * DB))
    out_ref[...] = jnp.where((rows > 0) & (columns > 0), (own + other) * rows * columns, 0.0)


def local(grad_out, acts, lengths):
    grads = grad_out.reshape(DB, KO, SEQ)
    inputs = acts.reshape(DB, SEQ, KI)
    dma = pltpu.SemaphoreType.DMA
    return pl.pallas_call(
        body,
        out_shape=jax.ShapeDtypeStruct((DB, 4 * DB), F32),
        in_specs=[
            pl.BlockSpec(memory_space=pltpu.SMEM),
            pl.BlockSpec(memory_space=pl.ANY),
            pl.BlockSpec(memory_space=pl.ANY),
        ],
        out_specs=pl.BlockSpec(memory_space=pltpu.VMEM),
        scratch_shapes=[
            pltpu.VMEM((DB, KO, SEQ), BF16),
            pltpu.VMEM((DB, SEQ, KI), BF16),
            pltpu.VMEM((DB * KO, KI), F32),
            pltpu.VMEM((4, 4, GO, DB, KI), BF16),
            pltpu.VMEM((14, GO, DB, KI), BF16),
            pltpu.VMEM((8, 8, PR, KI), F32),
            pltpu.VMEM((8, 8, PR, KI), F32),
            pltpu.VMEM((8, PR, KI), F32),
            pltpu.VMEM((8, PR, KI), F32),
            pltpu.VMEM((8, PR, KI), F32),
            pltpu.VMEM((4, 2, PR, KI), F32),
            pltpu.VMEM((8, PR, KI), F32),
            pltpu.VMEM((8, KI), F32),
            pltpu.VMEM((7, 8, KI), F32),
            pltpu.VMEM((8, KI), F32),
            pltpu.VMEM((4, 8, KI), F32),
            dma((2, DB // CH)),
            dma((7,)), dma((7,)),
            dma((4,)), dma((4,)),
            dma((2, 4, 2)), dma((2, 4, 2)),
            dma((4,)), dma((4,)),
            dma((2, 4)), dma((2, 4)),
            dma((8, 8)), dma((8, 8)),
            dma((8,)), dma((8,)),
            dma((8,)), dma((8,)),
            dma((4, 2)), dma((8,)),
        ],
        compiler_params=pltpu.CompilerParams(
            collective_id=0, has_side_effects=True, vmem_limit_bytes=62 * 2**20
        ),
    )(lengths, grads, inputs)


def solution(mesh):
    placed = (P("docs", "layer", None, None), P("docs", "layer", None, None), P("docs"))
    return jax.shard_map(
        local, mesh=mesh, in_specs=placed, out_specs=P("docs", "layer"), check_vma=False
    )
```

time: 91.6 us -> 80.4 us (0.88)
  Pallas kernels: 88.7 us -> 78.1 us
  local copies, waits for them, and re-layouts: 2.84 us -> 1.64 us
    pallas_call x1, Pallas kernels: 88.7 us -> 78.1 us  [local(): pl.pallas_call(body, out_shape=jax.ShapeDtypeStruct((DB, 4 * DB), F32), i...]
    unnamed x5 -> x1, local copies, waits for them, and re-layouts: 2.84 us -> 1.64 us
where the time goes in v2:
time: 80.4 us; the launch traced here: 79.7 us
  Pallas kernels  78.1 us (97%)
  local copies, waits for them, and re-layouts  1.64 us (2%)
    pallas_call x1, Pallas kernels, local(): pl.pallas_call(body, out_shape=jax.ShapeDtypeStruct((DB, 4 * DB), F32), i...  78.1 us
    unnamed x1, local copies, waits for them, and re-layouts  1.64 us

profile of v2, /device:TPU:16, one launch (start us, length us, event | category | flops | bytes accessed | tf_op | source)
XLA Modules:
  0.0 79.7 jit_solution(15013804246988166174)
XLA Ops:
  0.0 78.1 %shard_map.37 = f32[112,448]{1,0:T(8,128)} custom-call(s32[112]{0:T(128)} %lengths_ref.1, bf16[112,32,256]{2,1,0:T(8,128)(2,1)} %bitcast.3, bf16[112,256,128]{2,1,0:T(8,128)(2,1)} %bitcast.2), custom_call_target="tpu_custom_call" | custom-call | tf_op jit(solution)/shard_map/pallas_call | solution.py:416
  78.1 1.6 %copy.5 = f32[112,448]{1,0:T(8,128)} copy(f32[112,448]{1,0:T(8,128)} %shard_map.37) | data formatting | bytes 401408

commit v3 on v2

--- a/solution.py
+++ b/solution.py
@@ -41,7 +41,12 @@
     down = dev(lax.rem(z + NZ - 1, NZ), me, me_l)
     ypart = dev(z, yme, me_l)
     cpart = dev(z, yl * 2 + 1 - c, me_l)
-    self_final = (me_l // 2) == me
+    def owner(piece):
+        pair, to = piece // 4, piece % 4
+        return 4 * ((pair + to) % 2) + to
+
+    mine = 4 * ((yh + x) % 2) + x
+    self_final = (mine // 2) == me
     diagonal = me_l == z
 
     def rcopy(src, dst, ss, rs_, to):
@@ -70,7 +75,7 @@
         hello(dev(z, me, lax.rem(me_l + p, NZ)))
     @pl.loop(0, 8)
     def _(i):
-        ll = 2 * me + i // 4
+        ll = owner(2 * me + i // 4)
         slot = i % 4
         @pl.when(jnp.logical_not((ll == me_l) & (slot == me)))
         def _():
@@ -124,12 +129,13 @@
 
     order = (0, 2, 1, 3)
     acc = jnp.zeros((DB, KI), F32)
-    for kc in order:
+    for kc in range(4):
         for j in range(GO):
             values = feat[pl.ds(kc * GO + j, DB, stride=KO), :]
             acc = acc + values * values
             S[kc, me, j] = values.astype(BF16)
         z_copy(1, kc % 2, kc // 2).start()
+        y_copy(kc).start()
         c_copy(0, kc).start()
 
     eye = lax.broadcasted_iota(jnp.int32, (DB, KI), 0) == lax.broadcasted_iota(jnp.int32, (DB, KI), 1)
@@ -145,8 +151,6 @@
     @pl.loop(1, NZ)
     def _(p):
         sq_copy(p).start()
-    for kc in order:
-        y_copy(kc).start()
     PP[...] = jnp.zeros_like(PP)
     @pl.when(diagonal)
     def _():
@@ -182,6 +186,19 @@
         res = lax.dot_general(left, right, (((1,), (1,)), ((), ())), preferred_element_type=F32)
         return res.reshape(4, PR, KI)
 
+    def product_all(kc, xs):
+        right = jnp.concatenate([xs[j] for j in range(GO)], axis=1)
+        right = jnp.concatenate([right, jnp.zeros((KI - DB, GO * KI), BF16)], axis=0)
+        left = jnp.concatenate(
+            [jnp.concatenate([S[kc, r, j] for j in range(GO)], axis=1) for r in range(4)], axis=0
+        )
+        res = lax.dot_general(left, right, (((1,), (1,)), ((), ())), preferred_element_type=F32)
+        return res.reshape(8, PR, KI)
+
+    def multiply_all(i):
+        h1, sub, direction = i // 4, (i // 2) % 2, i % 2
+        PP[2 * h1 + direction] += product_all(direction * 2 + sub, R.at[i])
+
     def multiply(i, pair):
         h1, sub, direction = i // 4, (i // 2) % 2, i % 2
         PP[2 * h1 + direction, pl.ds(4 * pair, 4)] += product(direction * 2 + sub, R.at[i], pair)
@@ -190,12 +207,14 @@
         PP[7, pl.ds(4 * pair, 4)] += product(kc, S.at[kc, me], pair)
 
     def r_copy(b, to):
-        return rcopy(PP.at[b, to], RR.at[b, me_l], rs.at[b, to], rr.at[b, me_l], dev(z, me, to))
+        return rcopy(
+            PP.at[b, 4 * ((to // 4 + to) % 2) + to % 4], RR.at[b, me_l], rs.at[b, to], rr.at[b, me_l], dev(z, me, to)
+        )
 
     def send_partials(b, pair):
         @pl.loop(0, 4)
         def _(q):
-            to = 4 * pair + q
+            to = owner(4 * pair + q)
             @pl.when(to != me_l)
             def _():
                 r_copy(b, to).start()
@@ -220,10 +239,11 @@
             slot = 4 * pair + lax.rem(x + p, 4)
             rcopy(PP.at[b, 0], RR.at[b, slot], rs.at[b, 0], rr.at[b, slot], up).wait_recv()
             total = total + RR[b, slot]
-        @pl.when(pair == yh)
+        keep = yh == (pair + x) % 2
+        @pl.when(keep)
         def _():
             V[b] = total
-        @pl.when(pair != yh)
+        @pl.when(jnp.logical_not(keep))
         def _():
             XS[b] = total
             p_copy(b).start()
@@ -234,13 +254,13 @@
         return lax.rem(jnp.where(b == 7, z, jnp.where(b == 6, z + 4, other)), NZ)
 
     def l_copy(b):
-        return rcopy(V.at[b], L.at[me, me_l % 2], ls.at[b], lr.at[me, me_l % 2], dev(z, me_l // 2, plane_of(b)))
+        return rcopy(V.at[b], L.at[me, mine % 2], ls.at[b], lr.at[me, mine % 2], dev(z, mine // 2, plane_of(b)))
 
     def l_copy_self(b):
-        return pltpu.make_async_copy(V.at[b], L.at[me, me_l % 2], lr.at[me, me_l % 2])
+        return pltpu.make_async_copy(V.at[b], L.at[me, mine % 2], lr.at[me, mine % 2])
 
     def t_copy(b):
-        return rcopy(V.at[b], T.at[me_l], ts.at[b], tr.at[me_l], dev(plane_of(b), me, z))
+        return rcopy(V.at[b], T.at[mine], ts.at[b], tr.at[mine], dev(plane_of(b), me, z))
 
     def send_own(b):
         to_self = self_final & (plane_of(b) == me_l)
@@ -254,10 +274,9 @@
     def add_two_steps(b):
         p_copy(b).wait_recv()
         V[b] = V[b] + RY[b]
-        send_own(b)
 
     def add_up(b):
-        total = PP[b, me_l]
+        total = PP[b, mine]
         for p in range(1, NZ):
             source = lax.rem(me_l + p, NZ)
             rcopy(PP.at[b, 0], RR.at[b, source], rs.at[b, 0], rr.at[b, source], up).wait_recv()
@@ -280,8 +299,8 @@
                 def _():
                     z_copy(4, sub, direction).start()
         if tick < 4:
-            y_copy(order[tick]).wait_recv()
-            c_copy(1, order[tick]).start()
+            y_copy(tick).wait_recv()
+            c_copy(1, tick).start()
 
     for kc in order:
         c_copy(0, kc).wait_recv()
@@ -296,8 +315,11 @@
     @pl.loop(0, 2)
     def _(b):
         send_over_x(b, yl)
-    make_norms()
     pass_on(2)
+    for kc in range(2):
+        c_copy(1, kc).wait_recv()
+        multiply(2 * kc, 1 - yl)
+    send_over_x(0, 1 - yl)
     pass_on(3)
     @pl.loop(4, 8)
     def _(i):
@@ -305,33 +327,36 @@
     @pl.loop(2, 4)
     def _(b):
         send_over_x(b, yl)
-    for kc in order:
+    @pl.loop(0, 2)
+    def _(sub):
+        multiply(4 + 2 * sub, 1 - yl)
+    send_over_x(2, 1 - yl)
+    for kc in range(2, 4):
         c_copy(1, kc).wait_recv()
-    for kc in order:
+    @pl.loop(0, 2)
+    def _(h1):
+        @pl.loop(0, 2)
+        def _(sub):
+            multiply(4 * h1 + 2 * sub + 1, 1 - yl)
+        send_over_x(2 * h1 + 1, 1 - yl)
+    for kc in range(4):
         multiply_own(kc, 1 - yl)
     send_over_x(7, 1 - yl)
+    make_norms()
+    pass_on(4)
+    @pl.loop(8, 10)
+    def _(i):
+        multiply_all(i)
+    add_over_x(7, yl)
+    @pl.loop(0, 4)
+    def _(b):
+        add_over_x(b, yl)
+    pass_on(5)
     @pl.loop(0, 2)
-    def _(h1):
-        @pl.loop(0, 4)
-        def _(i):
-            multiply(4 * h1 + i, 1 - yl)
-        send_over_x(2 * h1, 1 - yl)
-        send_over_x(2 * h1 + 1, 1 - yl)
-    add_over_x(7, yl)
-    @pl.loop(0, 4)
-    def _(b):
-        add_over_x(b, yl)
-    pass_on(4)
-    @pl.loop(0, 4)
-    def _(i):
-        multiply(8 + i // 2, i % 2)
-    pass_on(5)
-    @pl.loop(0, 4)
-    def _(i):
-        multiply(10 + i // 2, i % 2)
-    @pl.loop(0, 4)
-    def _(i):
-        send_partials(4 + i // 2, i % 2)
+    def _(i):
+        multiply_all(10 + i)
+        send_partials(4 + i, 0)
+        send_partials(4 + i, 1)
 
     add_over_x(7, 1 - yl)
     @pl.loop(0, 4)
@@ -344,17 +369,11 @@
 
     for direction in range(2):
         z_copy(4, 0, direction).wait_recv()
-    for pair in range(2):
-        for direction in range(2):
-            PP[6, pl.ds(4 * pair, 4)] += product(direction * 2 + arriving, R.at[12 + direction], pair)
-        send_partials(6, pair)
-    @pl.loop(0, 4)
-    def _(b):
-        t_copy(b).start()
-    @pl.loop(4, 7)
-    def _(b):
-        add_up(b)
-
+    @pl.loop(0, 2)
+    def _(direction):
+        PP[6] += product_all(direction * 2 + arriving, R.at[12 + direction])
+    send_partials(6, 0)
+    send_partials(6, 1)
     for h in range(1, 5):
         for sub in range(2 if h < 4 else 1):
             for direction in range(2):
@@ -364,35 +383,28 @@
         c_copy(0, kc).wait_send()
         c_copy(1, kc).wait_send()
     other_slots(lambda t: norm_copy(t).wait_send())
-    @pl.loop(0, 8)
-    def _(b):
-        direct = (b >= 4) & (b < 7)
-        @pl.when(direct)
-        def _():
-            @pl.loop(0, NZ)
-            def _(to):
-                @pl.when(to != me_l)
-                def _():
-                    r_copy(b, to).wait_send()
-        @pl.when(jnp.logical_not(direct))
-        def _():
-            @pl.loop(0, NZ)
-            def _(i):
-                @pl.when(i % 4 != x)
-                def _():
-                    x_copy(b, i // 4, i % 4).wait_send()
-            p_copy(b).wait_send()
-        to_self = self_final & (plane_of(b) == me_l)
-        @pl.when(jnp.logical_not(to_self))
-        def _():
-            l_copy(b).wait_send()
-        @pl.when(b != 7)
-        def _():
-            t_copy(b).wait_send()
-
     def norm_arrived(t):
         rcopy(norm, norms.at[t], ns.at[t], nr.at[t], up).wait_recv()
     other_slots(norm_arrived)
+    @pl.loop(0, 5)
+    def _(i):
+        b = jnp.where(i == 4, 7, i)
+        @pl.loop(0, NZ)
+        def _(to):
+            @pl.when(to % 4 != x)
+            def _():
+                x_copy(b, to // 4, to % 4).wait_send()
+        p_copy(b).wait_send()
+
+    @pl.loop(4, 7)
+    def _(b):
+        add_up(b)
+    send_own(7)
+    @pl.loop(0, 4)
+    def _(b):
+        send_own(b)
+        t_copy(b).start()
+
     for t in range(4):
         for half in range(2):
             rcopy(V.at[0], L.at[t, half], ls.at[0], lr.at[t, half], up).wait_recv()
@@ -407,6 +419,23 @@
     columns = jnp.concatenate([norms[t, 0:1, :DB] for t in range(4)], axis=1)
     columns = jnp.broadcast_to(columns, (DB, 4 * DB))
     out_ref[...] = jnp.where((rows > 0) & (columns > 0), (own + other) * rows * columns, 0.0)
+
+    @pl.loop(0, 8)
+    def _(b):
+        @pl.when((b >= 4) & (b < 7))
+        def _():
+            @pl.loop(0, NZ)
+            def _(to):
+                @pl.when(to != me_l)
+                def _():
+                    r_copy(b, to).wait_send()
+        to_self = self_final & (plane_of(b) == me_l)
+        @pl.when(jnp.logical_not(to_self))
+        def _():
+            l_copy(b).wait_send()
+        @pl.when(b != 7)
+        def _():
+            t_copy(b).wait_send()
 
 
 def local(grad_out, acts, lengths):

time: 80.4 us -> 74 us (0.920)
  Pallas kernels: 78.1 us -> 71.6 us
    pallas_call x1, Pallas kernels: 78.1 us -> 71.6 us  [local(): pl.pallas_call(body, out_shape=jax.ShapeDtypeStruct((DB, 4 * DB), F32), i...]
where the time goes in v3:
time: 74 us; the launch traced here: 73.2 us
  Pallas kernels  71.6 us (97%)
  local copies, waits for them, and re-layouts  1.64 us (2%)
    pallas_call x1, Pallas kernels, local(): pl.pallas_call(body, out_shape=jax.ShapeDtypeStruct((DB, 4 * DB), F32), i...  71.6 us
    unnamed x1, local copies, waits for them, and re-layouts  1.64 us

profile of v3, /device:TPU:16, one launch (start us, length us, event | category | flops | bytes accessed | tf_op | source)
XLA Modules:
  0.0 73.2 jit_solution(13950983925738869769)
XLA Ops:
  0.0 71.6 %shard_map.37 = f32[112,448]{1,0:T(8,128)} custom-call(s32[112]{0:T(128)} %lengths_ref.1, bf16[112,32,256]{2,1,0:T(8,128)(2,1)} %bitcast.3, bf16[112,256,128]{2,1,0:T(8,128)(2,1)} %bitcast.2), custom_call_target="tpu_custom_call" | custom-call | tf_op jit(solution)/shard_map/pallas_call | solution.py:445
  71.6 1.6 %copy.5 = f32[112,448]{1,0:T(8,128)} copy(f32[112,448]{1,0:T(8,128)} %shard_map.37) | data formatting | bytes 401408

commit v4 on v3

--- a/solution.py
+++ b/solution.py
@@ -24,8 +24,8 @@
 
 def body(
     lengths_ref, grad_hbm, acts_hbm, out_ref,
-    gbuf, abuf, feat, S, R, PP, RR, XS, RY, V, L, T, sq, sqr, norm, norms,
-    in_sem, qs, qr, ns, nr, zs, zr, ys, yr, cs, cr, rs, rr, ps, pr, ls, ts, lr, tr,
+    gbuf, abuf, feat, S, R, PP, RR, XS, RY, RH, V, L, T, sq, sqr, norm, norms,
+    in_sem, qs, qr, ns, nr, zs, zr, ys, yr, cs, cr, rs, rr, ps, pr, hs, hr, ls, ts, lr, tr,
 ):
     d = lax.axis_index("docs")
     me_l = lax.axis_index("layer")
@@ -45,7 +45,8 @@
         pair, to = piece // 4, piece % 4
         return 4 * ((pair + to) % 2) + to
 
-    mine = 4 * ((yh + x) % 2) + x
+    my_pair = (yh + x) % 2
+    mine = 4 * my_pair + x
     self_final = (mine // 2) == me
     diagonal = me_l == z
 
@@ -129,14 +130,20 @@
 
     order = (0, 2, 1, 3)
     acc = jnp.zeros((DB, KI), F32)
-    for kc in range(4):
+    for i, kc in enumerate(order):
         for j in range(GO):
             values = feat[pl.ds(kc * GO + j, DB, stride=KO), :]
             acc = acc + values * values
             S[kc, me, j] = values.astype(BF16)
         z_copy(1, kc % 2, kc // 2).start()
-        y_copy(kc).start()
         c_copy(0, kc).start()
+        if i == 1:
+            y_copy(0).start()
+        if i == 2:
+            y_copy(1).start()
+            y_copy(2).start()
+        if i == 3:
+            y_copy(3).start()
 
     eye = lax.broadcasted_iota(jnp.int32, (DB, KI), 0) == lax.broadcasted_iota(jnp.int32, (DB, KI), 1)
     def as_column(row):
@@ -262,6 +269,53 @@
     def t_copy(b):
         return rcopy(V.at[b], T.at[mine], ts.at[b], tr.at[mine], dev(plane_of(b), me, z))
 
+    def h_copy(b, pair, j):
+        piece = 4 * pair + (pair + yh + 1) % 2 + 2 * j
+        return rcopy(
+            PP.at[b, piece], RH.at[b, pair, j], hs.at[b, pair, j], hr.at[b, pair, j], dev(z, me, 4 * (1 - yh) + x)
+        )
+
+    def send_over_y(b, pair):
+        for j in range(2):
+            h_copy(b, pair, j).start()
+
+    def add_over_y(b, pair):
+        for j in range(2):
+            to = (pair + yh) % 2 + 2 * j
+            h_copy(b, pair, j).wait_recv()
+            PP[b, 4 * pair + to] += RH[b, pair, j]
+            @pl.when(to != x)
+            def _():
+                x_copy(b, pair, to).start()
+
+    def over_y_left(b, pair):
+        for j in range(2):
+            to = (pair + yh) % 2 + 2 * j
+            h_copy(b, pair, j).wait_send()
+            @pl.when(to != x)
+            def _():
+                x_copy(b, pair, to).wait_send()
+
+    def over_x_left(b, pair):
+        @pl.loop(1, 4)
+        def _(p):
+            x_copy(b, pair, lax.rem(x + p, 4)).wait_send()
+        @pl.when(my_pair != pair)
+        def _():
+            p_copy(b).wait_send()
+
+    def finish_x(b):
+        p_copy(b).wait_recv()
+        V[b] = V[b] + RY[b]
+
+    def finish_y(b):
+        total = PP[b, mine]
+        for p in range(1, 4):
+            slot = 4 * my_pair + lax.rem(x + p, 4)
+            rcopy(PP.at[b, 0], RR.at[b, slot], rs.at[b, 0], rr.at[b, slot], up).wait_recv()
+            total = total + RR[b, slot]
+        V[b] = total
+
     def send_own(b):
         to_self = self_final & (plane_of(b) == me_l)
         @pl.when(to_self)
@@ -270,10 +324,6 @@
         @pl.when(jnp.logical_not(to_self))
         def _():
             l_copy(b).start()
-
-    def add_two_steps(b):
-        p_copy(b).wait_recv()
-        V[b] = V[b] + RY[b]
 
     def add_up(b):
         total = PP[b, mine]
@@ -282,8 +332,6 @@
             rcopy(PP.at[b, 0], RR.at[b, source], rs.at[b, 0], rr.at[b, source], up).wait_recv()
             total = total + RR[b, source]
         V[b] = total
-        send_own(b)
-        t_copy(b).start()
 
     far = (lax.rem(z + NZ - 3, NZ) // 4, lax.rem(z + 3, NZ) // 4)
     arriving = lax.rem(z + 4, NZ) // 4
@@ -324,13 +372,12 @@
     @pl.loop(4, 8)
     def _(i):
         multiply(i, yl)
-    @pl.loop(2, 4)
-    def _(b):
-        send_over_x(b, yl)
+    send_over_y(2, yl)
+    send_over_y(3, yl)
     @pl.loop(0, 2)
     def _(sub):
         multiply(4 + 2 * sub, 1 - yl)
-    send_over_x(2, 1 - yl)
+    send_over_y(2, 1 - yl)
     for kc in range(2, 4):
         c_copy(1, kc).wait_recv()
     @pl.loop(0, 2)
@@ -338,34 +385,36 @@
         @pl.loop(0, 2)
         def _(sub):
             multiply(4 * h1 + 2 * sub + 1, 1 - yl)
-        send_over_x(2 * h1 + 1, 1 - yl)
+        @pl.when(h1 == 0)
+        def _():
+            send_over_x(1, 1 - yl)
+        @pl.when(h1 == 1)
+        def _():
+            send_over_y(3, 1 - yl)
     for kc in range(4):
         multiply_own(kc, 1 - yl)
     send_over_x(7, 1 - yl)
+    add_over_x(7, yl)
+    add_over_x(0, yl)
+    add_over_x(1, yl)
+    add_over_x(0, 1 - yl)
     make_norms()
     pass_on(4)
     @pl.loop(8, 10)
     def _(i):
         multiply_all(i)
-    add_over_x(7, yl)
-    @pl.loop(0, 4)
-    def _(b):
-        add_over_x(b, yl)
+    add_over_y(2, yl)
+    add_over_y(3, yl)
+    add_over_y(2, 1 - yl)
     pass_on(5)
     @pl.loop(0, 2)
     def _(i):
         multiply_all(10 + i)
         send_partials(4 + i, 0)
         send_partials(4 + i, 1)
-
+    add_over_y(3, 1 - yl)
+    add_over_x(1, 1 - yl)
     add_over_x(7, 1 - yl)
-    @pl.loop(0, 4)
-    def _(b):
-        add_over_x(b, 1 - yl)
-    add_two_steps(7)
-    @pl.loop(0, 4)
-    def _(b):
-        add_two_steps(b)
 
     for direction in range(2):
         z_copy(4, 0, direction).wait_recv()
@@ -386,24 +435,55 @@
     def norm_arrived(t):
         rcopy(norm, norms.at[t], ns.at[t], nr.at[t], up).wait_recv()
     other_slots(norm_arrived)
-    @pl.loop(0, 5)
-    def _(i):
-        b = jnp.where(i == 4, 7, i)
-        @pl.loop(0, NZ)
-        def _(to):
-            @pl.when(to % 4 != x)
-            def _():
-                x_copy(b, to // 4, to % 4).wait_send()
-        p_copy(b).wait_send()
-
-    @pl.loop(4, 7)
+    over_x_left(7, yl)
+    over_x_left(0, yl)
+    over_x_left(1, yl)
+    over_x_left(0, 1 - yl)
+    for pair in (yl, 1 - yl):
+        over_y_left(2, pair)
+        over_y_left(3, pair)
+    over_x_left(1, 1 - yl)
+    over_x_left(7, 1 - yl)
+
+    finish_x(0)
+    finish_x(1)
+    finish_y(2)
+    finish_y(3)
+    finish_x(7)
+    @pl.loop(4, 6)
     def _(b):
         add_up(b)
+    add_up(6)
+    t_copy(6).start()
+    send_own(6)
+    @pl.loop(4, 6)
+    def _(b):
+        t_copy(b).start()
+        send_own(b)
+    @pl.loop(0, 4)
+    def _(b):
+        t_copy(b).start()
     send_own(7)
     @pl.loop(0, 4)
     def _(b):
         send_own(b)
-        t_copy(b).start()
+
+    @pl.loop(0, 8)
+    def _(b):
+        @pl.when((b >= 4) & (b < 7))
+        def _():
+            @pl.loop(0, NZ)
+            def _(to):
+                @pl.when(to != me_l)
+                def _():
+                    r_copy(b, to).wait_send()
+        to_self = self_final & (plane_of(b) == me_l)
+        @pl.when(jnp.logical_not(to_self))
+        def _():
+            l_copy(b).wait_send()
+        @pl.when(b != 7)
+        def _():
+            t_copy(b).wait_send()
 
     for t in range(4):
         for half in range(2):
@@ -419,23 +499,6 @@
     columns = jnp.concatenate([norms[t, 0:1, :DB] for t in range(4)], axis=1)
     columns = jnp.broadcast_to(columns, (DB, 4 * DB))
     out_ref[...] = jnp.where((rows > 0) & (columns > 0), (own + other) * rows * columns, 0.0)
-
-    @pl.loop(0, 8)
-    def _(b):
-        @pl.when((b >= 4) & (b < 7))
-        def _():
-            @pl.loop(0, NZ)
-            def _(to):
-                @pl.when(to != me_l)
-                def _():
-                    r_copy(b, to).wait_send()
-        to_self = self_final & (plane_of(b) == me_l)
-        @pl.when(jnp.logical_not(to_self))
-        def _():
-            l_copy(b).wait_send()
-        @pl.when(b != 7)
-        def _():
-            t_copy(b).wait_send()
 
 
 def local(grad_out, acts, lengths):
@@ -461,6 +524,7 @@
             pltpu.VMEM((8, 8, PR, KI), F32),
             pltpu.VMEM((8, PR, KI), F32),
             pltpu.VMEM((8, PR, KI), F32),
+            pltpu.VMEM((8, 2, 2, PR, KI), F32),
             pltpu.VMEM((8, PR, KI), F32),
             pltpu.VMEM((4, 2, PR, KI), F32),
             pltpu.VMEM((8, PR, KI), F32),
@@ -476,6 +540,7 @@
             dma((2, 4)), dma((2, 4)),
             dma((8, 8)), dma((8, 8)),
             dma((8,)), dma((8,)),
+            dma((8, 2, 2)), dma((8, 2, 2)),
             dma((8,)), dma((8,)),
             dma((4, 2)), dma((8,)),
         ],

time: 74 us -> 69.1 us (0.934)
  Pallas kernels: 71.6 us -> 66.1 us
    pallas_call x1, Pallas kernels: 71.6 us -> 66.1 us  [local(): pl.pallas_call(body, out_shape=jax.ShapeDtypeStruct((DB, 4 * DB), F32), i...]
where the time goes in v4:
time: 69.1 us; the launch traced here: 67.8 us
  Pallas kernels  66.1 us (96%)
  local copies, waits for them, and re-layouts  1.64 us (2%)
    pallas_call x1, Pallas kernels, local(): pl.pallas_call(body, out_shape=jax.ShapeDtypeStruct((DB, 4 * DB), F32), i...  66.1 us
    unnamed x1, local copies, waits for them, and re-layouts  1.64 us

profile of v4, /device:TPU:16, one launch (start us, length us, event | category | flops | bytes accessed | tf_op | source)
XLA Modules:
  0.0 67.8 jit_solution(12494570302650552123)
XLA Ops:
  0.0 66.1 %shard_map.37 = f32[112,448]{1,0:T(8,128)} custom-call(s32[112]{0:T(128)} %lengths_ref.1, bf16[112,32,256]{2,1,0:T(8,128)(2,1)} %bitcast.3, bf16[112,256,128]{2,1,0:T(8,128)(2,1)} %bitcast.2), custom_call_target="tpu_custom_call" | custom-call | tf_op jit(solution)/shard_map/pallas_call | solution.py:508
  66.1 1.6 %copy.5 = f32[112,448]{1,0:T(8,128)} copy(f32[112,448]{1,0:T(8,128)} %shard_map.37) | data formatting | bytes 401408

commit v5 on v4

--- a/solution.py
+++ b/solution.py
@@ -390,7 +390,7 @@
             send_over_x(1, 1 - yl)
         @pl.when(h1 == 1)
         def _():
-            send_over_y(3, 1 - yl)
+            send_over_x(3, 1 - yl)
     for kc in range(4):
         multiply_own(kc, 1 - yl)
     send_over_x(7, 1 - yl)
@@ -412,7 +412,7 @@
         multiply_all(10 + i)
         send_partials(4 + i, 0)
         send_partials(4 + i, 1)
-    add_over_y(3, 1 - yl)
+    add_over_x(3, 1 - yl)
     add_over_x(1, 1 - yl)
     add_over_x(7, 1 - yl)
 
@@ -441,14 +441,20 @@
     over_x_left(0, 1 - yl)
     for pair in (yl, 1 - yl):
         over_y_left(2, pair)
-        over_y_left(3, pair)
+    over_y_left(3, yl)
+    over_x_left(3, 1 - yl)
     over_x_left(1, 1 - yl)
     over_x_left(7, 1 - yl)
 
     finish_x(0)
     finish_x(1)
     finish_y(2)
-    finish_y(3)
+    @pl.when(my_pair == yl)
+    def _():
+        finish_y(3)
+    @pl.when(my_pair != yl)
+    def _():
+        finish_x(3)
     finish_x(7)
     @pl.loop(4, 6)
     def _(b):

time: 69.1 us -> 69 us (level)
  no operation moved by 1% of the time
where the time goes in v5:
time: 69 us; the launch traced here: 67.7 us
  Pallas kernels  66 us (96%)
  local copies, waits for them, and re-layouts  1.64 us (2%)
    pallas_call x1, Pallas kernels, local(): pl.pallas_call(body, out_shape=jax.ShapeDtypeStruct((DB, 4 * DB), F32), i...  66 us
    unnamed x1, local copies, waits for them, and re-layouts  1.64 us

profile of v5, /device:TPU:16, one launch (start us, length us, event | category | flops | bytes accessed | tf_op | source)
XLA Modules:
  0.0 67.7 jit_solution(12924497776637670447)
XLA Ops:
  0.0 66.0 %shard_map.37 = f32[112,448]{1,0:T(8,128)} custom-call(s32[112]{0:T(128)} %lengths_ref.1, bf16[112,32,256]{2,1,0:T(8,128)(2,1)} %bitcast.3, bf16[112,256,128]{2,1,0:T(8,128)(2,1)} %bitcast.2), custom_call_target="tpu_custom_call" | custom-call | tf_op jit(solution)/shard_map/pallas_call | solution.py:514
  66.0 1.6 %copy.5 = f32[112,448]{1,0:T(8,128)} copy(f32[112,448]{1,0:T(8,128)} %shard_map.37) | data formatting | bytes 401408
